TPU v7x, 32 devices: a whole 2x2x4 slice. The times are simulated.
32 devices in a mesh: gx: 2 (over x), gy: 2 (over y), gz: 8 (over z, core).
Axes of the slice: x: 2, y: 2, z: 4, core: 2. Of those that a mesh axis runs over, the one named last changes fastest.
Arguments:
- seeds: float32 [2, 2, 8, 64, 256], P('gx', 'gy', 'gz'), may hold values from -6 to 6
- schur: float32 [2, 2, 8, 1152, 1152], P('gx', 'gy', 'gz')
- inverse: float32 [2, 2, 8, 1152, 1152], P('gx', 'gy', 'gz')
- deluxe: float32 [2, 2, 8, 1152], P('gx', 'gy', 'gz'), may hold values from 0.5 to 2
- orders: int32 [2, 2, 8], P('gx', 'gy', 'gz'), may hold values from 360 to 1152, as said below
- links: int32 [2, 2, 8, 1152], P('gx', 'gy', 'gz'), may hold values from 0 to 1791, as said below
Outputs:
- adjoint: float32 [2, 2, 8, 64, 256], P('gx', 'gy', 'gz')
- residual: float32 [2, 2, 8, 64, 256], P('gx', 'gy', 'gz')
Inputs may be any that keep to these rules, and one draw needn't show every extreme that they name: `orders`: each value lies in 360 to 1152; some subdomain has exactly 1152. `links`: A slot names only a subdomain that exists in the grid; entries at rows at or beyond the subdomain's order are arbitrary.
All inputs are finite; a program needn't handle non-finite values.
Results may differ from a plain program's by a relative error of at most 0.00015.
Values sent between devices are 32-bit elements; how exact they have to be, the bound alone decides.
A program may use at most 64 MiB of HBM per device.

v0:
```python
import jax
import jax.numpy as jnp
from jax import lax
from jax.sharding import PartitionSpec as P


def extended(array, sides, width):
    for axis, dim in sides:
        peers, length = (lax.axis_size(axis), array.shape[dim])
        up = [(i, (i + 1) % peers) for i in range(peers - 1)]
        down = [(j, i) for i, j in up]
        last = lax.slice_in_dim(array, length - width, length, axis=dim)
        leading = lax.slice_in_dim(array, 0, width, axis=dim)
        before = lax.ppermute(last, axis, up)
        after = lax.ppermute(leading, axis, down)
        array = jnp.concatenate([before, array, after], axis=dim)
    return array


def shifted(value, axis, steps):
    count = lax.axis_size(axis)
    leading, last = (max(0, -steps), min(count, count - steps))
    return lax.ppermute(value, axis, [(source, source + steps) for source in range(leading, last)])


def gather_pool(block):
    padded = extended(block[None, None, None], (("gx", 0), ("gy", 1), ("gz", 2)), 1)
    pieces = [
        padded[1, 1, 1],
        padded[0, 1, 1],
        padded[2, 1, 1],
        padded[1, 0, 1],
        padded[1, 2, 1],
        padded[1, 1, 0],
        padded[1, 1, 2],
    ]
    return jnp.concatenate(pieces, axis=1)


def return_sums(contrib, owned):

    def piece(slot):
        return contrib[:, slot * owned : (slot + 1) * owned]

    total = piece(0)
    for offset, slot in ((1, 2), (-1, 1)):
        total = total + shifted(piece(slot), "gx", offset)
    for offset, slot in ((1, 4), (-1, 3)):
        total = total + shifted(piece(slot), "gy", offset)
    for offset, slot in ((1, 6), (-1, 5)):
        total = total + shifted(piece(slot), "gz", offset)
    return total


def apply_local(block, matrix, weight, rows):
    owned = block.shape[1]
    pool = gather_pool(block)
    local = jnp.take(pool, rows, axis=1) * weight[None, :]
    image = (
        jnp.dot(local, matrix, precision=lax.Precision.HIGHEST, preferred_element_type=jnp.float32)
        * weight[None, :]
    )
    contrib = jnp.zeros((block.shape[0], 7 * owned), jnp.float32).at[:, rows].add(image)
    return return_sums(contrib, owned)


def body(seeds, schur, inverse, deluxe, orders, links):
    order_count = schur.shape[3]
    gradient = seeds[0, 0, 0]
    rows = links[0, 0, 0]
    mask = (jnp.arange(order_count, dtype=jnp.int32) < orders.reshape(())).astype(jnp.float32)
    weight = mask * deluxe[0, 0, 0]
    schur_local = schur[0, 0, 0]
    inverse_local = inverse[0, 0, 0]
    adjoint1 = apply_local(gradient, inverse_local, weight, rows)
    residual = gradient - apply_local(adjoint1, schur_local, mask, rows)
    adjoint = adjoint1 + apply_local(residual, inverse_local, weight, rows)
    return (adjoint[None, None, None], residual[None, None, None])


def solution(mesh):
    in_specs = (
        P("gx", "gy", "gz", None, None),
        P("gx", "gy", "gz", None, None),
        P("gx", "gy", "gz", None, None),
        P("gx", "gy", "gz", None),
        P("gx", "gy", "gz"),
        P("gx", "gy", "gz", None),
    )
    out_specs = (P("gx", "gy", "gz", None, None), P("gx", "gy", "gz", None, None))
    return jax.shard_map(body, mesh=mesh, in_specs=in_specs, out_specs=out_specs, check_vma=False)
```

profile of v0, /device:TPU:0, one launch (start us, length us, event | category | flops | bytes accessed | tf_op | source)
XLA Modules:
  0.0 237.5 jit_solution(13282437848119945826)
XLA Ops:
  1.6 4.8 %collective-permute-start = (f32[1,1,1,64,256]{3,4,2,1,0:T(8,128)S(1)}, f32[1,1,1,64,256]{3,4,2,1,0:T(8,128)S(1)}, u32[]{:S(2)}, u32[]{:S(2)}) collective-permute-start(f32[1,1,1,64,256]{3,4,2,1,0:T(8,128)S(1)} %copy.32), channel_id=1, source_target_pairs={{0,16},{1,17},{2,18},{3,19},{4,20},{5,21},{6,22},{7,23},{8,24},{9,... | collective-permute-start | bytes 196616 | tf_op jit(solution)/shard_map/ppermute | solution.py:14
  18.1 5.6 %collective-permute-done.2 = f32[3,1,1,64,256]{3,4,2,1,0:T(8,128)S(1)} collective-permute-done((f32[3,1,1,64,256]{3,4,2,1,0:T(8,128)S(1)}, f32[3,1,1,64,256]{3,4,2,1,0:T(8,128)S(1)}, u32[]{:S(2)}, u32[]{:S(2)}) %collective-permute-start.2) | collective-permute-done | bytes 196640 | tf_op jit(solution)/shard_map/ppermute | solution.py:14
  23.7 4.1 %collective-permute-done.3 = f32[3,1,1,64,256]{3,4,2,1,0:T(8,128)S(1)} collective-permute-done((f32[3,1,1,64,256]{3,4,2,1,0:T(8,128)S(1)}, f32[3,1,1,64,256]{3,4,2,1,0:T(8,128)S(1)}, u32[]{:S(2)}, u32[]{:S(2)}) %collective-permute-start.3) | collective-permute-done | bytes 196640 | tf_op jit(solution)/shard_map/ppermute | solution.py:15
  39.1 5.4 %fusion.21 = f32[1152,64]{0,1:T(8,128)S(1)} fusion(f32[1,1,1,1152,1152]{4,3,2,1,0:T(8,128)} %param.10, f32[1152,64]{0,1:T(8,128)S(1)} %copy.40, f32[1152]{0:T(1024)S(1)} %fusion.67, pred[1152]{0:T(1024)(128)(4,1)S(1)} %get-tuple-element.32), kind=kOutput, calls=%fused_computation.17 | convolution fusion | flops 1019437056 | bytes 5904000 | tf_op jit(solution)/shard_map/dot_general | solution.py:60
  44.8 9.1 %scatter_custom_fusion = f32[64,1792]{0,1:T(8,128)S(1)} fusion(s32[1152]{0:T(1024)S(1)} %fusion.68, f32[1152,64]{1,0:T(8,128)S(1)} %copy.41, f32[]{:T(128)} %constant.3.clone.1), kind=kCustom, calls=%fused_computation.25 | custom fusion | flops 73728 | bytes 458756 | tf_op jit(solution)/shard_map/scatter-add | solution.py:63
  55.2 10.3 %collective-permute-start.10 = (f32[64,256]{0,1:T(8,128)S(1)}, f32[64,256]{0,1:T(8,128)S(1)}, u32[]{:S(2)}, u32[]{:S(2)}) collective-permute-start(f32[64,256]{0,1:T(8,128)S(1)} %get-tuple-element.27), channel_id=1, source_target_pairs={{0,1},{1,2},{2,3},{3,4},{4,5},{5,6},{6,7},{8,9},{9,10},{10,11},{11... | collective-permute-start | bytes 196616 | tf_op jit(solution)/shard_map/ppermute | solution.py:23
  66.9 4.6 %collective-permute-start.8 = (f32[64,256]{0,1:T(8,128)S(1)}, f32[64,256]{0,1:T(8,128)S(1)}, u32[]{:S(2)}, u32[]{:S(2)}) collective-permute-start(f32[64,256]{0,1:T(8,128)S(1)} %get-tuple-element.29), channel_id=1, source_target_pairs={{0,8},{1,9},{2,10},{3,11},{4,12},{5,13},{6,14},{7,15},{16,24},{17,... | collective-permute-start | bytes 196616 | tf_op jit(solution)/shard_map/ppermute | solution.py:23
  72.7 4.6 %collective-permute-start.6 = (f32[64,256]{0,1:T(8,128)S(1)}, f32[64,256]{0,1:T(8,128)S(1)}, u32[]{:S(2)}, u32[]{:S(2)}) collective-permute-start(f32[64,256]{0,1:T(8,128)S(1)} %get-tuple-element.25), channel_id=1, source_target_pairs={{0,16},{1,17},{2,18},{3,19},{4,20},{5,21},{6,22},{7,23},{8,24},{9,... | collective-permute-start | bytes 196616 | tf_op jit(solution)/shard_map/ppermute | solution.py:23
  81.1 4.4 %collective-permute-start.12 = (f32[1,1,1,64,256]{3,4,2,1,0:T(8,128)S(1)}, f32[1,1,1,64,256]{3,4,2,1,0:T(8,128)S(1)}, u32[]{:S(2)}, u32[]{:S(2)}) collective-permute-start(f32[1,1,1,64,256]{3,4,2,1,0:T(8,128)S(1)} %bitcast.96), channel_id=1, source_target_pairs={{0,16},{1,17},{2,18},{3,19},{4,20},{5,21},{6,22},{7,23},{8,24},{9,... | collective-permute-start | bytes 196616 | tf_op jit(solution)/shard_map/ppermute | solution.py:14
  95.3 6.3 %collective-permute-done.14 = f32[3,1,1,64,256]{3,4,2,1,0:T(8,128)S(1)} collective-permute-done((f32[3,1,1,64,256]{3,4,2,1,0:T(8,128)S(1)}, f32[3,1,1,64,256]{3,4,2,1,0:T(8,128)S(1)}, u32[]{:S(2)}, u32[]{:S(2)}) %collective-permute-start.14) | collective-permute-done | bytes 196640 | tf_op jit(solution)/shard_map/ppermute | solution.py:14
  101.6 4.1 %collective-permute-done.15 = f32[3,1,1,64,256]{3,4,2,1,0:T(8,128)S(1)} collective-permute-done((f32[3,1,1,64,256]{3,4,2,1,0:T(8,128)S(1)}, f32[3,1,1,64,256]{3,4,2,1,0:T(8,128)S(1)}, u32[]{:S(2)}, u32[]{:S(2)}) %collective-permute-start.15) | collective-permute-done | bytes 196640 | tf_op jit(solution)/shard_map/ppermute | solution.py:15
  116.9 5.4 %fusion.15 = f32[1152,64]{0,1:T(8,128)S(1)} fusion(f32[1,1,1,1152,1152]{4,3,2,1,0:T(8,128)} %param.9, f32[1152,64]{0,1:T(8,128)S(1)} %copy.46, f32[1152]{0:T(1024)S(1)} %get-tuple-element.31, pred[1152]{0:T(1024)(128)(4,1)S(1)} %get-tuple-element.32), kind=kOutput, calls=%fused_computation.15 | convolution fusion | flops 1019437056 | bytes 5904000 | tf_op jit(solution)/shard_map/dot_general | solution.py:60
  122.6 9.1 %scatter_custom_fusion.1 = f32[64,1792]{0,1:T(8,128)S(1)} fusion(s32[1152]{0:T(1024)S(1)} %fusion.68, f32[1152,64]{1,0:T(8,128)S(1)} %copy.47, f32[]{:T(128)} %constant.3.clone.1), kind=kCustom, calls=%fused_computation.23 | custom fusion | flops 73728 | bytes 458756 | tf_op jit(solution)/shard_map/scatter-add | solution.py:63
  133.0 10.3 %collective-permute-start.22 = (f32[64,256]{0,1:T(8,128)S(1)}, f32[64,256]{0,1:T(8,128)S(1)}, u32[]{:S(2)}, u32[]{:S(2)}) collective-permute-start(f32[64,256]{0,1:T(8,128)S(1)} %get-tuple-element.21), channel_id=1, source_target_pairs={{0,1},{1,2},{2,3},{3,4},{4,5},{5,6},{6,7},{8,9},{9,10},{10,11},{11... | collective-permute-start | bytes 196616 | tf_op jit(solution)/shard_map/ppermute | solution.py:23
  144.7 4.6 %collective-permute-start.20 = (f32[64,256]{0,1:T(8,128)S(1)}, f32[64,256]{0,1:T(8,128)S(1)}, u32[]{:S(2)}, u32[]{:S(2)}) collective-permute-start(f32[64,256]{0,1:T(8,128)S(1)} %get-tuple-element.23), channel_id=1, source_target_pairs={{0,8},{1,9},{2,10},{3,11},{4,12},{5,13},{6,14},{7,15},{16,24},{17,... | collective-permute-start | bytes 196616 | tf_op jit(solution)/shard_map/ppermute | solution.py:23
  150.5 4.6 %collective-permute-start.18 = (f32[64,256]{0,1:T(8,128)S(1)}, f32[64,256]{0,1:T(8,128)S(1)}, u32[]{:S(2)}, u32[]{:S(2)}) collective-permute-start(f32[64,256]{0,1:T(8,128)S(1)} %get-tuple-element.19), channel_id=1, source_target_pairs={{0,16},{1,17},{2,18},{3,19},{4,20},{5,21},{6,22},{7,23},{8,24},{9,... | collective-permute-start | bytes 196616 | tf_op jit(solution)/shard_map/ppermute | solution.py:23
  159.0 4.4 %collective-permute-start.24 = (f32[1,1,1,64,256]{3,4,2,1,0:T(8,128)S(1)}, f32[1,1,1,64,256]{3,4,2,1,0:T(8,128)S(1)}, u32[]{:S(2)}, u32[]{:S(2)}) collective-permute-start(f32[1,1,1,64,256]{3,4,2,1,0:T(8,128)S(1)} %bitcast.100), channel_id=1, source_target_pairs={{0,16},{1,17},{2,18},{3,19},{4,20},{5,21},{6,22},{7,23},{8,24},{9,... | collective-permute-start | bytes 196616 | tf_op jit(solution)/shard_map/ppermute | solution.py:14
  173.1 6.3 %collective-permute-done.26 = f32[3,1,1,64,256]{3,4,2,1,0:T(8,128)S(1)} collective-permute-done((f32[3,1,1,64,256]{3,4,2,1,0:T(8,128)S(1)}, f32[3,1,1,64,256]{3,4,2,1,0:T(8,128)S(1)}, u32[]{:S(2)}, u32[]{:S(2)}) %collective-permute-start.26) | collective-permute-done | bytes 196640 | tf_op jit(solution)/shard_map/ppermute | solution.py:14
  179.4 4.1 %collective-permute-done.27 = f32[3,1,1,64,256]{3,4,2,1,0:T(8,128)S(1)} collective-permute-done((f32[3,1,1,64,256]{3,4,2,1,0:T(8,128)S(1)}, f32[3,1,1,64,256]{3,4,2,1,0:T(8,128)S(1)}, u32[]{:S(2)}, u32[]{:S(2)}) %collective-permute-start.27) | collective-permute-done | bytes 196640 | tf_op jit(solution)/shard_map/ppermute | solution.py:15
  194.7 5.4 %fusion.18 = f32[1152,64]{0,1:T(8,128)S(1)} fusion(f32[1,1,1,1152,1152]{4,3,2,1,0:T(8,128)} %param.10, f32[1152,64]{0,1:T(8,128)S(1)} %copy.52, f32[1152]{0:T(1024)S(1)} %fusion.67, pred[1152]{0:T(1024)(128)(4,1)S(1)} %get-tuple-element.32), kind=kOutput, calls=%fused_computation.16 | convolution fusion | flops 1019437056 | bytes 5904000 | tf_op jit(solution)/shard_map/dot_general | solution.py:60
  200.4 9.1 %scatter_custom_fusion.2 = f32[64,1792]{0,1:T(8,128)S(1)} fusion(s32[1152]{0:T(1024)S(1)} %fusion.68, f32[1152,64]{1,0:T(8,128)S(1)} %copy.53, f32[]{:T(128)} %constant.3.clone.1), kind=kCustom, calls=%fused_computation.21 | custom fusion | flops 73728 | bytes 458756 | tf_op jit(solution)/shard_map/scatter-add | solution.py:63
  210.8 10.3 %collective-permute-start.34 = (f32[64,256]{0,1:T(8,128)S(1)}, f32[64,256]{0,1:T(8,128)S(1)}, u32[]{:S(2)}, u32[]{:S(2)}) collective-permute-start(f32[64,256]{0,1:T(8,128)S(1)} %get-tuple-element.15), channel_id=1, source_target_pairs={{0,1},{1,2},{2,3},{3,4},{4,5},{5,6},{6,7},{8,9},{9,10},{10,11},{11... | collective-permute-start | bytes 196616 | tf_op jit(solution)/shard_map/ppermute | solution.py:23
  222.5 4.6 %collective-permute-start.32 = (f32[64,256]{0,1:T(8,128)S(1)}, f32[64,256]{0,1:T(8,128)S(1)}, u32[]{:S(2)}, u32[]{:S(2)}) collective-permute-start(f32[64,256]{0,1:T(8,128)S(1)} %get-tuple-element.17), channel_id=1, source_target_pairs={{0,8},{1,9},{2,10},{3,11},{4,12},{5,13},{6,14},{7,15},{16,24},{17,... | collective-permute-start | bytes 196616 | tf_op jit(solution)/shard_map/ppermute | solution.py:23
  228.4 4.6 %collective-permute-start.30 = (f32[64,256]{0,1:T(8,128)S(1)}, f32[64,256]{0,1:T(8,128)S(1)}, u32[]{:S(2)}, u32[]{:S(2)}) collective-permute-start(f32[64,256]{0,1:T(8,128)S(1)} %get-tuple-element.13), channel_id=1, source_target_pairs={{0,16},{1,17},{2,18},{3,19},{4,20},{5,21},{6,22},{7,23},{8,24},{9,... | collective-permute-start | bytes 196616 | tf_op jit(solution)/shard_map/ppermute | solution.py:23
  (119 shorter events, 89.4 us)
Async XLA Ops:
  1.6 9.0 %collective-permute-start = (f32[1,1,1,64,256]{3,4,2,1,0:T(8,128)S(1)}, f32[1,1,1,64,256]{3,4,2,1,0:T(8,128)S(1)}, u32[]{:S(2)}, u32[]{:S(2)}) collective-permute-start(f32[1,1,1,64,256]{3,4,2,1,0:T(8,128)S(1)} %copy.32), channel_id=1, source_target_pairs={{0,16},{1,17},{2,18},{3,19},{4,20},{5,21},{6,22},{7,23},{8,24},{9,... | collective-permute-start | bytes 196616 | tf_op jit(solution)/shard_map/ppermute | solution.py:14
  13.3 10.4 %collective-permute-start.2 = (f32[3,1,1,64,256]{3,4,2,1,0:T(8,128)S(1)}, f32[3,1,1,64,256]{3,4,2,1,0:T(8,128)S(1)}, u32[]{:S(2)}, u32[]{:S(2)}) collective-permute-start(f32[3,1,1,64,256]{3,4,2,1,0:T(8,128)S(1)} %pad_maximum_fusion.3), channel_id=1, source_target_pairs={{0,8},{1,9},{2,10},{3,11},{4,12},{5,13},{6,14},{7,15},{16,24},{17,... | collective-permute-start | bytes 589832 | tf_op jit(solution)/shard_map/ppermute | solution.py:14
  16.8 11.0 %collective-permute-start.3 = (f32[3,1,1,64,256]{3,4,2,1,0:T(8,128)S(1)}, f32[3,1,1,64,256]{3,4,2,1,0:T(8,128)S(1)}, u32[]{:S(2)}, u32[]{:S(2)}) collective-permute-start(f32[3,1,1,64,256]{3,4,2,1,0:T(8,128)S(1)} %pad_maximum_fusion.3), channel_id=1, source_target_pairs={{8,0},{9,1},{10,2},{11,3},{12,4},{13,5},{14,6},{15,7},{24,16},{25,... | collective-permute-start | bytes 589832 | tf_op jit(solution)/shard_map/ppermute | solution.py:15
  53.9 18.8 %collective-permute-start.11 = (f32[64,256]{0,1:T(8,128)S(1)}, f32[64,256]{0,1:T(8,128)S(1)}, u32[]{:S(2)}, u32[]{:S(2)}) collective-permute-start(f32[64,256]{0,1:T(8,128)S(1)} %get-tuple-element.26), channel_id=1, source_target_pairs={{1,0},{2,1},{3,2},{4,3},{5,4},{6,5},{7,6},{9,8},{10,9},{11,10},{12... | collective-permute-start | bytes 196616 | tf_op jit(solution)/shard_map/ppermute | solution.py:23
  55.2 22.1 %collective-permute-start.10 = (f32[64,256]{0,1:T(8,128)S(1)}, f32[64,256]{0,1:T(8,128)S(1)}, u32[]{:S(2)}, u32[]{:S(2)}) collective-permute-start(f32[64,256]{0,1:T(8,128)S(1)} %get-tuple-element.27), channel_id=1, source_target_pairs={{0,1},{1,2},{2,3},{3,4},{4,5},{5,6},{6,7},{8,9},{9,10},{10,11},{11... | collective-permute-start | bytes 196616 | tf_op jit(solution)/shard_map/ppermute | solution.py:23
  65.6 11.8 %collective-permute-start.9 = (f32[64,256]{0,1:T(8,128)S(1)}, f32[64,256]{0,1:T(8,128)S(1)}, u32[]{:S(2)}, u32[]{:S(2)}) collective-permute-start(f32[64,256]{0,1:T(8,128)S(1)} %get-tuple-element.28), channel_id=1, source_target_pairs={{8,0},{9,1},{10,2},{11,3},{12,4},{13,5},{14,6},{15,7},{24,16},{25,... | collective-permute-start | bytes 196616 | tf_op jit(solution)/shard_map/ppermute | solution.py:23
  66.9 10.5 %collective-permute-start.8 = (f32[64,256]{0,1:T(8,128)S(1)}, f32[64,256]{0,1:T(8,128)S(1)}, u32[]{:S(2)}, u32[]{:S(2)}) collective-permute-start(f32[64,256]{0,1:T(8,128)S(1)} %get-tuple-element.29), channel_id=1, source_target_pairs={{0,8},{1,9},{2,10},{3,11},{4,12},{5,13},{6,14},{7,15},{16,24},{17,... | collective-permute-start | bytes 196616 | tf_op jit(solution)/shard_map/ppermute | solution.py:23
  71.4 8.1 %collective-permute-start.7 = (f32[64,256]{0,1:T(8,128)S(1)}, f32[64,256]{0,1:T(8,128)S(1)}, u32[]{:S(2)}, u32[]{:S(2)}) collective-permute-start(f32[64,256]{0,1:T(8,128)S(1)} %get-tuple-element.30), channel_id=1, source_target_pairs={{16,0},{17,1},{18,2},{19,3},{20,4},{21,5},{22,6},{23,7},{24,8},{25... | collective-permute-start | bytes 196616 | tf_op jit(solution)/shard_map/ppermute | solution.py:23
  72.7 8.4 %collective-permute-start.6 = (f32[64,256]{0,1:T(8,128)S(1)}, f32[64,256]{0,1:T(8,128)S(1)}, u32[]{:S(2)}, u32[]{:S(2)}) collective-permute-start(f32[64,256]{0,1:T(8,128)S(1)} %get-tuple-element.25), channel_id=1, source_target_pairs={{0,16},{1,17},{2,18},{3,19},{4,20},{5,21},{6,22},{7,23},{8,24},{9,... | collective-permute-start | bytes 196616 | tf_op jit(solution)/shard_map/ppermute | solution.py:23
  92.6 9.0 %collective-permute-start.14 = (f32[3,1,1,64,256]{3,4,2,1,0:T(8,128)S(1)}, f32[3,1,1,64,256]{3,4,2,1,0:T(8,128)S(1)}, u32[]{:S(2)}, u32[]{:S(2)}) collective-permute-start(f32[3,1,1,64,256]{3,4,2,1,0:T(8,128)S(1)} %pad_maximum_fusion.4), channel_id=1, source_target_pairs={{0,8},{1,9},{2,10},{3,11},{4,12},{5,13},{6,14},{7,15},{16,24},{17,... | collective-permute-start | bytes 589832 | tf_op jit(solution)/shard_map/ppermute | solution.py:14
  93.9 11.8 %collective-permute-start.15 = (f32[3,1,1,64,256]{3,4,2,1,0:T(8,128)S(1)}, f32[3,1,1,64,256]{3,4,2,1,0:T(8,128)S(1)}, u32[]{:S(2)}, u32[]{:S(2)}) collective-permute-start(f32[3,1,1,64,256]{3,4,2,1,0:T(8,128)S(1)} %pad_maximum_fusion.4), channel_id=1, source_target_pairs={{8,0},{9,1},{10,2},{11,3},{12,4},{13,5},{14,6},{15,7},{24,16},{25,... | collective-permute-start | bytes 589832 | tf_op jit(solution)/shard_map/ppermute | solution.py:15
  131.7 18.8 %collective-permute-start.23 = (f32[64,256]{0,1:T(8,128)S(1)}, f32[64,256]{0,1:T(8,128)S(1)}, u32[]{:S(2)}, u32[]{:S(2)}) collective-permute-start(f32[64,256]{0,1:T(8,128)S(1)} %get-tuple-element.20), channel_id=1, source_target_pairs={{1,0},{2,1},{3,2},{4,3},{5,4},{6,5},{7,6},{9,8},{10,9},{11,10},{12... | collective-permute-start | bytes 196616 | tf_op jit(solution)/shard_map/ppermute | solution.py:23
  133.0 22.1 %collective-permute-start.22 = (f32[64,256]{0,1:T(8,128)S(1)}, f32[64,256]{0,1:T(8,128)S(1)}, u32[]{:S(2)}, u32[]{:S(2)}) collective-permute-start(f32[64,256]{0,1:T(8,128)S(1)} %get-tuple-element.21), channel_id=1, source_target_pairs={{0,1},{1,2},{2,3},{3,4},{4,5},{5,6},{6,7},{8,9},{9,10},{10,11},{11... | collective-permute-start | bytes 196616 | tf_op jit(solution)/shard_map/ppermute | solution.py:23
  143.4 11.8 %collective-permute-start.21 = (f32[64,256]{0,1:T(8,128)S(1)}, f32[64,256]{0,1:T(8,128)S(1)}, u32[]{:S(2)}, u32[]{:S(2)}) collective-permute-start(f32[64,256]{0,1:T(8,128)S(1)} %get-tuple-element.22), channel_id=1, source_target_pairs={{8,0},{9,1},{10,2},{11,3},{12,4},{13,5},{14,6},{15,7},{24,16},{25,... | collective-permute-start | bytes 196616 | tf_op jit(solution)/shard_map/ppermute | solution.py:23
  144.7 10.5 %collective-permute-start.20 = (f32[64,256]{0,1:T(8,128)S(1)}, f32[64,256]{0,1:T(8,128)S(1)}, u32[]{:S(2)}, u32[]{:S(2)}) collective-permute-start(f32[64,256]{0,1:T(8,128)S(1)} %get-tuple-element.23), channel_id=1, source_target_pairs={{0,8},{1,9},{2,10},{3,11},{4,12},{5,13},{6,14},{7,15},{16,24},{17,... | collective-permute-start | bytes 196616 | tf_op jit(solution)/shard_map/ppermute | solution.py:23
  149.2 8.1 %collective-permute-start.19 = (f32[64,256]{0,1:T(8,128)S(1)}, f32[64,256]{0,1:T(8,128)S(1)}, u32[]{:S(2)}, u32[]{:S(2)}) collective-permute-start(f32[64,256]{0,1:T(8,128)S(1)} %get-tuple-element.24), channel_id=1, source_target_pairs={{16,0},{17,1},{18,2},{19,3},{20,4},{21,5},{22,6},{23,7},{24,8},{25... | collective-permute-start | bytes 196616 | tf_op jit(solution)/shard_map/ppermute | solution.py:23
  150.5 8.4 %collective-permute-start.18 = (f32[64,256]{0,1:T(8,128)S(1)}, f32[64,256]{0,1:T(8,128)S(1)}, u32[]{:S(2)}, u32[]{:S(2)}) collective-permute-start(f32[64,256]{0,1:T(8,128)S(1)} %get-tuple-element.19), channel_id=1, source_target_pairs={{0,16},{1,17},{2,18},{3,19},{4,20},{5,21},{6,22},{7,23},{8,24},{9,... | collective-permute-start | bytes 196616 | tf_op jit(solution)/shard_map/ppermute | solution.py:23
  170.4 9.0 %collective-permute-start.26 = (f32[3,1,1,64,256]{3,4,2,1,0:T(8,128)S(1)}, f32[3,1,1,64,256]{3,4,2,1,0:T(8,128)S(1)}, u32[]{:S(2)}, u32[]{:S(2)}) collective-permute-start(f32[3,1,1,64,256]{3,4,2,1,0:T(8,128)S(1)} %pad_maximum_fusion.5), channel_id=1, source_target_pairs={{0,8},{1,9},{2,10},{3,11},{4,12},{5,13},{6,14},{7,15},{16,24},{17,... | collective-permute-start | bytes 589832 | tf_op jit(solution)/shard_map/ppermute | solution.py:14
  171.8 11.8 %collective-permute-start.27 = (f32[3,1,1,64,256]{3,4,2,1,0:T(8,128)S(1)}, f32[3,1,1,64,256]{3,4,2,1,0:T(8,128)S(1)}, u32[]{:S(2)}, u32[]{:S(2)}) collective-permute-start(f32[3,1,1,64,256]{3,4,2,1,0:T(8,128)S(1)} %pad_maximum_fusion.5), channel_id=1, source_target_pairs={{8,0},{9,1},{10,2},{11,3},{12,4},{13,5},{14,6},{15,7},{24,16},{25,... | collective-permute-start | bytes 589832 | tf_op jit(solution)/shard_map/ppermute | solution.py:15
  209.5 18.8 %collective-permute-start.35 = (f32[64,256]{0,1:T(8,128)S(1)}, f32[64,256]{0,1:T(8,128)S(1)}, u32[]{:S(2)}, u32[]{:S(2)}) collective-permute-start(f32[64,256]{0,1:T(8,128)S(1)} %get-tuple-element.14), channel_id=1, source_target_pairs={{1,0},{2,1},{3,2},{4,3},{5,4},{6,5},{7,6},{9,8},{10,9},{11,10},{12... | collective-permute-start | bytes 196616 | tf_op jit(solution)/shard_map/ppermute | solution.py:23
  210.8 22.8 %collective-permute-start.34 = (f32[64,256]{0,1:T(8,128)S(1)}, f32[64,256]{0,1:T(8,128)S(1)}, u32[]{:S(2)}, u32[]{:S(2)}) collective-permute-start(f32[64,256]{0,1:T(8,128)S(1)} %get-tuple-element.15), channel_id=1, source_target_pairs={{0,1},{1,2},{2,3},{3,4},{4,5},{5,6},{6,7},{8,9},{9,10},{10,11},{11... | collective-permute-start | bytes 196616 | tf_op jit(solution)/shard_map/ppermute | solution.py:23
  221.2 12.5 %collective-permute-start.33 = (f32[64,256]{0,1:T(8,128)S(1)}, f32[64,256]{0,1:T(8,128)S(1)}, u32[]{:S(2)}, u32[]{:S(2)}) collective-permute-start(f32[64,256]{0,1:T(8,128)S(1)} %get-tuple-element.16), channel_id=1, source_target_pairs={{8,0},{9,1},{10,2},{11,3},{12,4},{13,5},{14,6},{15,7},{24,16},{25,... | collective-permute-start | bytes 196616 | tf_op jit(solution)/shard_map/ppermute | solution.py:23
  222.5 11.2 %collective-permute-start.32 = (f32[64,256]{0,1:T(8,128)S(1)}, f32[64,256]{0,1:T(8,128)S(1)}, u32[]{:S(2)}, u32[]{:S(2)}) collective-permute-start(f32[64,256]{0,1:T(8,128)S(1)} %get-tuple-element.17), channel_id=1, source_target_pairs={{0,8},{1,9},{2,10},{3,11},{4,12},{5,13},{6,14},{7,15},{16,24},{17,... | collective-permute-start | bytes 196616 | tf_op jit(solution)/shard_map/ppermute | solution.py:23
  228.4 8.4 %collective-permute-start.30 = (f32[64,256]{0,1:T(8,128)S(1)}, f32[64,256]{0,1:T(8,128)S(1)}, u32[]{:S(2)}, u32[]{:S(2)}) collective-permute-start(f32[64,256]{0,1:T(8,128)S(1)} %get-tuple-element.13), channel_id=1, source_target_pairs={{0,16},{1,17},{2,18},{3,19},{4,20},{5,21},{6,22},{7,23},{8,24},{9,... | collective-permute-start | bytes 196616 | tf_op jit(solution)/shard_map/ppermute | solution.py:23
  (12 other events, 70.4 us)
where the time goes:
time: 239 us; the launch traced here: 237 us
  starting transfers between devices  106 us (44%)
  waiting for transfers between devices  68.1 us (28%)
  other arithmetic  29.9 us (13%)
  matrix products  16.3 us (7%)
  local copies, waits for them, and re-layouts  15.5 us (6%)
    ppermute x18, starting transfers between devices, shifted(): lax.ppermute(value, axis, [(source, source + steps) for source in range(l...  70 us
    ppermute x9, waiting for transfers between devices, extended(): after = lax.ppermute(leading, axis, down)  35.1 us
    scatter-add x3, other arithmetic, apply_local(): jnp.zeros((block.shape[0], 7 * owned), jnp.float32).at[:, rows].add(image)  27.2 us
    ppermute x9, starting transfers between devices, extended(): before = lax.ppermute(last, axis, up)  23.7 us
    ppermute x9, waiting for transfers between devices, extended(): before = lax.ppermute(last, axis, up)  22.4 us
    dot_general x3, matrix products, apply_local(): jnp.dot(local, matrix, precision=lax.Precision.HIGHEST, preferred_element...  16.3 us
    ppermute x9, starting transfers between devices, extended(): after = lax.ppermute(leading, axis, down)  12 us
    ppermute x18, waiting for transfers between devices, shifted(): lax.ppermute(value, axis, [(source, source + steps) for source in range(l...  10.6 us
  transfers between devices with their start and end apart: 36, of which 23 were waited for; matrix products, arithmetic and copies ran while one was open for 1% of the time, Pallas kernels for 0%

commit v1 on v0

v1 whole, which is shorter than its diff:
```python
import functools

import jax
import jax.numpy as jnp
from jax import lax
from jax.experimental import pallas as pl
from jax.experimental.pallas import tpu as pltpu
from jax.sharding import PartitionSpec as P

MESH = pl.DeviceIdType.MESH
F32 = jnp.float32
BF16 = jnp.bfloat16
AXES = ("gx", "gy", "gz")


def slot_plan(sizes):
    remote, kept = [], [0]
    for at, size in enumerate(sizes):
        here = 1 + len(remote)
        if size == 2:
            remote.append((at, 0, here))
            kept += [here, here]
        else:
            remote += [(at, -1, here + 1), (at, 1, here)]
            kept += [here, here + 1]
    return remote, kept


def split(value):
    high = value.astype(BF16)
    return high, (value - high.astype(F32)).astype(BF16)


def kernel(
    sizes,
    remote,
    kept,
    seeds,
    schur_hbm,
    inverse_hbm,
    deluxe_ref,
    order_ref,
    links_ref,
    adjoint_ref,
    residual_ref,
    schur,
    inverse,
    schur_high,
    schur_low,
    inverse_high,
    inverse_low,
    pick,
    landed,
    contrib,
    first,
    stacked,
    local,
    load_sem,
    send_sem,
    recv_sem,
):
    rows, owned = seeds.shape
    order_count = schur.shape[0]
    at = [lax.axis_index(name) for name in AXES]

    def neighbour(slot):
        axis, step, _ = remote[slot - 1]
        there = list(at)
        there[axis] = 1 - at[axis] if step == 0 else at[axis] + step
        return tuple(there)

    def present(slot, run, otherwise=None):
        axis, step, _ = remote[slot - 1]
        if step == 0:
            run()
            return
        there = at[axis] > 0 if step < 0 else at[axis] < sizes[axis] - 1
        pl.when(there)(run)
        if otherwise is not None:
            pl.when(jnp.logical_not(there))(otherwise)

    slots = range(1, len(remote) + 1)

    def copy_to(stage, slot, source):
        there = remote[slot - 1][2]
        return pltpu.make_async_remote_copy(
            src_ref=source,
            dst_ref=landed.at[stage, there - 1],
            send_sem=send_sem.at[stage, slot - 1],
            recv_sem=recv_sem.at[stage, there - 1],
            device_id=neighbour(slot),
            device_id_type=MESH,
        )

    def copy_from(stage, slot):
        return pltpu.make_async_remote_copy(
            src_ref=landed.at[stage, slot - 1],
            dst_ref=landed.at[stage, slot - 1],
            send_sem=send_sem.at[stage, slot - 1],
            recv_sem=recv_sem.at[stage, slot - 1],
            device_id=neighbour(slot),
            device_id_type=MESH,
        )

    load_inverse = pltpu.make_async_copy(inverse_hbm, inverse, load_sem.at[0])
    load_schur = pltpu.make_async_copy(schur_hbm, schur, load_sem.at[1])
    load_inverse.start()
    load_schur.start()

    barrier = pltpu.get_barrier_semaphore()
    for slot in slots:
        present(
            slot,
            lambda slot=slot: pl.semaphore_signal(
                barrier, inc=1, device_id=neighbour(slot), device_id_type=MESH
            ),
        )
    peers = 0
    for axis, step, _ in remote:
        if step == 0:
            peers += 1
        else:
            there = at[axis] > 0 if step < 0 else at[axis] < sizes[axis] - 1
            peers += jnp.where(there, 1, 0)
    pl.semaphore_wait(barrier, peers)

    def send_all(stage, source):
        for slot in slots:
            present(slot, lambda slot=slot: copy_to(stage, slot, source).start())

    send_all(0, seeds)

    for slot in slots:

        def clear(slot=slot):
            for stage in range(6):
                landed[stage, slot - 1] = jnp.zeros((rows, owned), F32)

        present(slot, lambda: None, clear)

    links = links_ref[0, 0]
    place = links
    for slot, here in enumerate(kept):
        if here != slot:
            inside = jnp.logical_and(links >= slot * owned, links < (slot + 1) * owned)
            place = jnp.where(inside, links + (here - slot) * owned, place)
    column = lax.broadcasted_iota(jnp.int32, (1, order_count), 1)
    place = jnp.where(column < order_ref[0, 0, 0], place, -1)
    index = lax.broadcasted_iota(jnp.int32, (owned, 1), 0)
    for slot in range(len(remote) + 1):
        pick[slot] = jnp.where(place == index + slot * owned, 1.0, 0.0).astype(BF16)
    weight = deluxe_ref[0, 0]

    def prepare(matrix, high, low):
        step = 128

        def some(i, carry):
            part = pl.ds(pl.multiple_of(i * step, step), step)
            high[part, :], low[part, :] = split(matrix[part, :])
            return carry

        lax.fori_loop(0, order_count // step, some, 0)

    def gather(stage, own):
        def add(slot, block):
            high, low = split(block)
            both = jnp.concatenate([high, low], axis=0)
            part = jnp.dot(both, pick[slot], preferred_element_type=F32)
            if slot == 0:
                local[...] = part
            else:
                local[...] += part

        add(0, own)
        for slot in reversed(slots):
            present(slot, lambda slot=slot: copy_from(stage, slot).wait_recv())
            add(slot, landed[stage, slot - 1])

    def apply(turn, own, high, low, scaled):
        gather(2 * turn, own)
        value = local[:rows] + local[rows:]
        if scaled:
            value = value * weight
        value_high, value_low = split(value)
        stacked[:rows] = value_high
        stacked[rows:] = value_low
        main = jnp.dot(stacked[...], high[...], preferred_element_type=F32)
        rest = jnp.dot(stacked[:rows], low[...], preferred_element_type=F32)
        image = main[:rows] + main[rows:] + rest
        if scaled:
            image = image * weight
        image_high, image_low = split(image)
        stacked[:rows] = image_high
        stacked[rows:] = image_low

        def scatter(slot):
            both = lax.dot_general(
                stacked[...], pick[slot], (((1,), (1,)), ((), ())), preferred_element_type=F32
            )
            return both[:rows] + both[rows:]

        for slot in slots:
            contrib[turn, slot - 1] = scatter(slot)
            present(
                slot,
                lambda slot=slot: copy_to(2 * turn + 1, slot, contrib.at[turn, slot - 1]).start(),
            )
        return scatter(0)

    def returned(turn, total):
        for slot in reversed(slots):
            present(slot, lambda slot=slot: copy_from(2 * turn + 1, slot).wait_recv())
            total = total + landed[2 * turn + 1, slot - 1]
        return total

    load_inverse.wait()
    prepare(inverse, inverse_high, inverse_low)
    own = apply(0, seeds[...], inverse_high, inverse_low, True)
    load_schur.wait()
    prepare(schur, schur_high, schur_low)
    first[...] = returned(0, own)
    send_all(2, first)

    own = apply(1, first[...], schur_high, schur_low, False)
    residual_ref[...] = seeds[...] - returned(1, own)
    send_all(4, residual_ref)

    own = apply(2, residual_ref[...], inverse_high, inverse_low, True)
    adjoint_ref[...] = first[...] + returned(2, own)

    for stage, source in enumerate((seeds, None, first, None, residual_ref, None)):
        for slot in slots:
            block = contrib.at[stage // 2, slot - 1] if source is None else source
            present(
                slot,
                lambda stage=stage, slot=slot, block=block: copy_to(stage, slot, block).wait_send(),
            )


def solution(mesh):
    sizes = tuple(mesh.shape[name] for name in AXES)
    remote, kept = slot_plan(sizes)

    def body(seeds, schur, inverse, deluxe, orders, links):
        rows, owned = seeds.shape[3:]
        order_count = schur.shape[3]
        count = len(remote)
        vmem = pl.BlockSpec(memory_space=pltpu.VMEM)
        hbm = pl.BlockSpec(memory_space=pl.ANY)
        result = jax.ShapeDtypeStruct((rows, owned), F32)
        square = (order_count, order_count)
        adjoint, residual = pl.pallas_call(
            functools.partial(kernel, sizes, remote, kept),
            out_shape=(result, result),
            in_specs=[vmem, hbm, hbm, vmem, pl.BlockSpec(memory_space=pltpu.SMEM), vmem],
            out_specs=(vmem, vmem),
            scratch_shapes=[
                pltpu.VMEM(square, F32),
                pltpu.VMEM(square, F32),
                pltpu.VMEM(square, BF16),
                pltpu.VMEM(square, BF16),
                pltpu.VMEM(square, BF16),
                pltpu.VMEM(square, BF16),
                pltpu.VMEM((count + 1, owned, order_count), BF16),
                pltpu.VMEM((6, count, rows, owned), F32),
                pltpu.VMEM((3, count, rows, owned), F32),
                pltpu.VMEM((rows, owned), F32),
                pltpu.VMEM((2 * rows, order_count), BF16),
                pltpu.VMEM((2 * rows, order_count), F32),
                pltpu.SemaphoreType.DMA((2,)),
                pltpu.SemaphoreType.DMA((6, count)),
                pltpu.SemaphoreType.DMA((6, count)),
            ],
            compiler_params=pltpu.CompilerParams(
                collective_id=0, has_side_effects=True, vmem_limit_bytes=60 * 1024 * 1024
            ),
        )(
            seeds[0, 0, 0],
            schur[0, 0, 0],
            inverse[0, 0, 0],
            deluxe[0],
            orders,
            links[0],
        )
        return adjoint[None, None, None], residual[None, None, None]

    in_specs = (
        P("gx", "gy", "gz", None, None),
        P("gx", "gy", "gz", None, None),
        P("gx", "gy", "gz", None, None),
        P("gx", "gy", "gz", None),
        P("gx", "gy", "gz"),
        P("gx", "gy", "gz", None),
    )
    out_specs = (P("gx", "gy", "gz", None, None), P("gx", "gy", "gz", None, None))
    return jax.shard_map(body, mesh=mesh, in_specs=in_specs, out_specs=out_specs, check_vma=False)
```

time: 239 us -> 38.3 us (0.16)
  starting transfers between devices: 106 us -> 0 us
  waiting for transfers between devices: 68.1 us -> 0 us
  Pallas kernels: 0 us -> 33.8 us
  other arithmetic: 29.9 us -> 0 us
  matrix products: 16.3 us -> 0 us
  local copies, waits for them, and re-layouts: 15.5 us -> 2.95 us
    ppermute x36 -> x0, starting transfers between devices: 106 us -> none  [the longest x18 70 us: shifted(): lax.ppermute(value, axis, [(source, source + steps) for source in range(l...]
    ppermute x36 -> x0, waiting for transfers between devices: 68.1 us -> none  [the longest x9 35.1 us: extended(): after = lax.ppermute(leading, axis, down)]
    pallas_call x0 -> x1, Pallas kernels: none -> 33.8 us  [body(): pl.pallas_call(functools.partial(kernel, sizes, remote, kept), out_shape=...]
    scatter-add x3 -> x0, other arithmetic: 27.2 us -> none  [apply_local(): jnp.zeros((block.shape[0], 7 * owned), jnp.float32).at[:, rows].add(image)]
    dot_general x3 -> x0, matrix products: 16.3 us -> none  [apply_local(): jnp.dot(local, matrix, precision=lax.Precision.HIGHEST, preferred_element...]
    gather x6 -> x0, local copies, waits for them, and re-layouts: 7.97 us -> none  [apply_local(): local = jnp.take(pool, rows, axis=1) * weight[None, :]]
    concatenate x6 -> x0, local copies, waits for them, and re-layouts: 3.58 us -> none  [the longest x3 3.54 us: extended(): array = jnp.concatenate([before, array, after], axis=dim)]
  transfers between devices with their start and end apart: 36 -> 0, of which waited for: 23 -> 0; matrix products, arithmetic and copies ran while one was open for 1% -> 0% of each run, Pallas kernels for 0% -> 0%
where the time goes in v1:
time: 38.3 us; the launch traced here: 38.1 us
  Pallas kernels  33.8 us (88%)
  local copies, waits for them, and re-layouts  2.95 us (8%)
  between operations  1.29 us (3%)
    pallas_call x1, Pallas kernels, body(): pl.pallas_call(functools.partial(kernel, sizes, remote, kept), out_shape=...  33.8 us
    unnamed x2, local copies, waits for them, and re-layouts  2.95 us

profile of v1, /device:TPU:0, one launch (start us, length us, event | category | flops | bytes accessed | tf_op | source)
XLA Modules:
  0.0 38.1 jit_solution(14086829810647061674)
XLA Ops:
  1.3 33.8 %shard_map.77 = (f32[64,256]{1,0:T(8,128)}, f32[64,256]{1,0:T(8,128)}) custom-call(f32[64,256]{1,0:T(8,128)} %bitcast.9, f32[1152,1152]{1,0:T(8,128)} %bitcast.7, f32[1152,1152]{1,0:T(8,128)} %bitcast.8, f32[1,1,1152]{2,1,0:T(1,128)} %bitcast.12, s32[1,1,1]{2,1,0:T(1,128)S(6)} %copy.10.order_ref, s32[1,1,1152]{2,1,0:T(1,128)} %bitcast.13), custom_call_target="tpu_custom_call" | custom-call | tf_op jit(solution)/shard_map/pallas_call | solution.py:252
  35.1 1.5 %copy.11 = f32[1,1,1,64,256]{4,3,2,1,0:T(8,128)} copy(f32[1,1,1,64,256]{4,3,2,1,0:T(8,128)} %bitcast.11) | data formatting | bytes 131072
  36.6 1.5 %copy.12 = f32[1,1,1,64,256]{4,3,2,1,0:T(8,128)} copy(f32[1,1,1,64,256]{4,3,2,1,0:T(8,128)} %bitcast.10) | data formatting | bytes 131072

commit v2 on v1

--- a/solution.py
+++ b/solution.py
@@ -50,10 +50,12 @@
     inverse_high,
     inverse_low,
     pick,
+    place_back,
     landed,
     contrib,
     first,
     stacked,
+    images,
     local,
     load_sem,
     send_sem,
@@ -61,6 +63,7 @@
 ):
     rows, owned = seeds.shape
     order_count = schur.shape[0]
+    wide = 384 if order_count % 384 == 0 else 128
     at = [lax.axis_index(name) for name in AXES]
 
     def neighbour(slot):
@@ -105,7 +108,6 @@
     load_inverse = pltpu.make_async_copy(inverse_hbm, inverse, load_sem.at[0])
     load_schur = pltpu.make_async_copy(schur_hbm, schur, load_sem.at[1])
     load_inverse.start()
-    load_schur.start()
 
     barrier = pltpu.get_barrier_semaphore()
     for slot in slots:
@@ -138,7 +140,7 @@
 
         present(slot, lambda: None, clear)
 
-    links = links_ref[0, 0]
+    links = links_ref[0]
     place = links
     for slot, here in enumerate(kept):
         if here != slot:
@@ -149,7 +151,15 @@
     index = lax.broadcasted_iota(jnp.int32, (owned, 1), 0)
     for slot in range(len(remote) + 1):
         pick[slot] = jnp.where(place == index + slot * owned, 1.0, 0.0).astype(BF16)
-    weight = deluxe_ref[0, 0]
+    weight = deluxe_ref[0]
+
+    def transpose_pick():
+        spread = jnp.broadcast_to(place.astype(F32), (128, order_count)).T.astype(jnp.int32)
+        lane = lax.broadcasted_iota(jnp.int32, (1, 128), 1)
+        for at_column in range(0, place_back.shape[1], 128):
+            found = jnp.where(spread == lane + at_column, 1.0, 0.0)
+            place_back[:, at_column : at_column + 128] = found.astype(BF16)
+
 
     def prepare(matrix, high, low):
         step = 128
@@ -184,19 +194,20 @@
         value_high, value_low = split(value)
         stacked[:rows] = value_high
         stacked[rows:] = value_low
-        main = jnp.dot(stacked[...], high[...], preferred_element_type=F32)
-        rest = jnp.dot(stacked[:rows], low[...], preferred_element_type=F32)
-        image = main[:rows] + main[rows:] + rest
-        if scaled:
-            image = image * weight
-        image_high, image_low = split(image)
-        stacked[:rows] = image_high
-        stacked[rows:] = image_low
+        for part in range(0, order_count, wide):
+            columns = slice(part, part + wide)
+            main = jnp.dot(stacked[...], high[:, columns], preferred_element_type=F32)
+            rest = jnp.dot(stacked[:rows], low[:, columns], preferred_element_type=F32)
+            image = main[:rows] + main[rows:] + rest
+            if scaled:
+                image = image * weight[:, columns]
+            image_high, image_low = split(image)
+            images[:rows, columns] = image_high
+            images[rows:, columns] = image_low
 
         def scatter(slot):
-            both = lax.dot_general(
-                stacked[...], pick[slot], (((1,), (1,)), ((), ())), preferred_element_type=F32
-            )
+            back = place_back[:, slot * owned : (slot + 1) * owned]
+            both = jnp.dot(images[...], back, preferred_element_type=F32)
             return both[:rows] + both[rows:]
 
         for slot in slots:
@@ -213,7 +224,9 @@
             total = total + landed[2 * turn + 1, slot - 1]
         return total
 
+    transpose_pick()
     load_inverse.wait()
+    load_schur.start()
     prepare(inverse, inverse_high, inverse_low)
     own = apply(0, seeds[...], inverse_high, inverse_low, True)
     load_schur.wait()
@@ -235,6 +248,15 @@
                 slot,
                 lambda stage=stage, slot=slot, block=block: copy_to(stage, slot, block).wait_send(),
             )
+
+
+def hand_over(adjoint, residual, adjoint_out, residual_out, sems):
+    one = pltpu.make_async_copy(adjoint, adjoint_out, sems.at[0])
+    two = pltpu.make_async_copy(residual, residual_out, sems.at[1])
+    one.start()
+    two.start()
+    one.wait()
+    two.wait()
 
 
 def solution(mesh):
@@ -262,9 +284,11 @@
                 pltpu.VMEM(square, BF16),
                 pltpu.VMEM(square, BF16),
                 pltpu.VMEM((count + 1, owned, order_count), BF16),
+                pltpu.VMEM((order_count, (count + 1) * owned), BF16),
                 pltpu.VMEM((6, count, rows, owned), F32),
                 pltpu.VMEM((3, count, rows, owned), F32),
                 pltpu.VMEM((rows, owned), F32),
+                pltpu.VMEM((2 * rows, order_count), BF16),
                 pltpu.VMEM((2 * rows, order_count), BF16),
                 pltpu.VMEM((2 * rows, order_count), F32),
                 pltpu.SemaphoreType.DMA((2,)),
@@ -282,6 +306,13 @@
             orders,
             links[0],
         )
+        adjoint, residual = pl.pallas_call(
+            hand_over,
+            out_shape=(result, result),
+            in_specs=[hbm, hbm],
+            out_specs=(hbm, hbm),
+            scratch_shapes=[pltpu.SemaphoreType.DMA((2,))],
+        )(adjoint, residual)
         return adjoint[None, None, None], residual[None, None, None]
 
     in_specs = (

time: 38.3 us -> 39.8 us (1.039)
  Pallas kernels: 33.8 us -> 38.3 us
  local copies, waits for them, and re-layouts: 2.95 us -> 0 us
    pallas_call x0 -> x1, Pallas kernels: none -> 5.09 us  [body(): pl.pallas_call(hand_over, out_shape=(result, result), in_specs=[hbm, hbm]...]
    unnamed x2 -> x0, local copies, waits for them, and re-layouts: 2.95 us -> none
    pallas_call x1, Pallas kernels: 33.8 us -> 33.3 us  [body(): pl.pallas_call(functools.partial(kernel, sizes, remote, kept), out_shape=...]
where the time goes in v2:
time: 39.8 us; the launch traced here: 39.6 us
  Pallas kernels  38.3 us (96%)
  between operations  1.29 us (3%)
    pallas_call x1, Pallas kernels, body(): pl.pallas_call(functools.partial(kernel, sizes, remote, kept), out_shape=...  33.3 us
    pallas_call x1, Pallas kernels, body(): pl.pallas_call(hand_over, out_shape=(result, result), in_specs=[hbm, hbm]...  5.09 us

profile of v2, /device:TPU:0, one launch (start us, length us, event | category | flops | bytes accessed | tf_op | source)
XLA Modules:
  0.0 39.6 jit_solution(16806962364005372390)
XLA Ops:
  1.3 33.3 %shard_map.77 = (f32[64,256]{1,0:T(8,128)}, f32[64,256]{1,0:T(8,128)}) custom-call(f32[64,256]{1,0:T(8,128)} %bitcast.9, f32[1152,1152]{1,0:T(8,128)} %bitcast.7, f32[1152,1152]{1,0:T(8,128)} %bitcast.8, f32[1,1,1152]{2,1,0:T(1,128)} %bitcast.10, s32[1,1,1]{2,1,0:T(1,128)S(6)} %copy.8.order_ref, s32[1,1,1152]{2,1,0:T(1,128)} %bitcast.11), custom_call_target="tpu_custom_call" | custom-call | tf_op jit(solution)/shard_map/pallas_call | solution.py:274
  34.5 5.1 %shard_map.78 = (f32[64,256]{1,0:T(8,128)}, f32[64,256]{1,0:T(8,128)}) custom-call(f32[64,256]{1,0:T(8,128)} %get-tuple-element.6.adjoint, f32[64,256]{1,0:T(8,128)} %get-tuple-element.7.residual), custom_call_target="tpu_custom_call" | custom-call | tf_op jit(solution)/shard_map/pallas_call | solution.py:309

commit v3 on v2

--- a/solution.py
+++ b/solution.py
@@ -250,13 +250,9 @@
             )
 
 
-def hand_over(adjoint, residual, adjoint_out, residual_out, sems):
-    one = pltpu.make_async_copy(adjoint, adjoint_out, sems.at[0])
-    two = pltpu.make_async_copy(residual, residual_out, sems.at[1])
-    one.start()
-    two.start()
-    one.wait()
-    two.wait()
+def hand_over(adjoint, residual, adjoint_out, residual_out):
+    adjoint_out[...] = adjoint[...]
+    residual_out[...] = residual[...]
 
 
 def solution(mesh):
@@ -309,9 +305,8 @@
         adjoint, residual = pl.pallas_call(
             hand_over,
             out_shape=(result, result),
-            in_specs=[hbm, hbm],
-            out_specs=(hbm, hbm),
-            scratch_shapes=[pltpu.SemaphoreType.DMA((2,))],
+            in_specs=[vmem, vmem],
+            out_specs=(vmem, vmem),
         )(adjoint, residual)
         return adjoint[None, None, None], residual[None, None, None]
 

time: 39.8 us -> 36.3 us (0.912)
  Pallas kernels: 38.3 us -> 34.8 us
    pallas_call x1, Pallas kernels: 5.09 us -> 1.53 us  [body(): pl.pallas_call(hand_over, out_shape=(result, result), in_specs=[vmem, vme...]
where the time goes in v3:
time: 36.3 us; the launch traced here: 36.1 us
  Pallas kernels  34.8 us (96%)
  between operations  1.29 us (4%)
    pallas_call x1, Pallas kernels, body(): pl.pallas_call(functools.partial(kernel, sizes, remote, kept), out_shape=...  33.3 us
    pallas_call x1, Pallas kernels, body(): pl.pallas_call(hand_over, out_shape=(result, result), in_specs=[vmem, vme...  1.53 us

profile of v3, /device:TPU:0, one launch (start us, length us, event | category | flops | bytes accessed | tf_op | source)
XLA Modules:
  0.0 36.1 jit_solution(2147663793485183981)
XLA Ops:
  1.3 33.3 %shard_map.77 = (f32[64,256]{1,0:T(8,128)}, f32[64,256]{1,0:T(8,128)}) custom-call(f32[64,256]{1,0:T(8,128)} %bitcast.9, f32[1152,1152]{1,0:T(8,128)} %bitcast.7, f32[1152,1152]{1,0:T(8,128)} %bitcast.8, f32[1,1,1152]{2,1,0:T(1,128)} %bitcast.10, s32[1,1,1]{2,1,0:T(1,128)S(6)} %copy.8.order_ref, s32[1,1,1152]{2,1,0:T(1,128)} %bitcast.11), custom_call_target="tpu_custom_call" | custom-call | tf_op jit(solution)/shard_map/pallas_call | solution.py:270
  34.5 1.5 %shard_map.78 = (f32[64,256]{1,0:T(8,128)}, f32[64,256]{1,0:T(8,128)}) custom-call(f32[64,256]{1,0:T(8,128)} %get-tuple-element.6.adjoint, f32[64,256]{1,0:T(8,128)} %get-tuple-element.7.residual), custom_call_target="tpu_custom_call" | custom-call | tf_op jit(solution)/shard_map/pallas_call | solution.py:305
